TPU v7x, 1024 devices: a whole 8x8x8 slice. The times are simulated.
1024 devices in a mesh: dp: 16 (over z, core), ep: 8 (over y), tp: 8 (over x).
Axes of the slice: x: 8, y: 8, z: 8, core: 2. Of those that a mesh axis runs over, the one named last changes fastest.
Arguments:
- grad_out: bfloat16 [4096, 7168], P(('dp', 'ep'), 'tp'), may hold values from -6 to 6
- expert_ids: int32 [4096, 4], P(('dp', 'ep')), may hold values from 0 to 7, all different within a row; in each aligned block of 32 rows (0 to 31, 32 to 63, ...) at most 32 rows name the same one
- gate_values: bfloat16 [4096, 4], P(('dp', 'ep')), may hold values from 0.099609375 to 1
- pre_gate: bfloat16 [8, 4096, 2048], P('ep', 'dp', 'tp'), may hold values from -8 to 8
- pre_up: bfloat16 [8, 4096, 2048], P('ep', 'dp', 'tp'), may hold values from -6 to 6
- down_weight: bfloat16 [8, 2048, 7168], P('ep', 'tp'), may hold values from -0.125 to 0.125
Outputs:
- grad_pre_gate: bfloat16 [8, 4096, 2048], P('ep', 'dp', 'tp')
- grad_pre_up: bfloat16 [8, 4096, 2048], P('ep', 'dp', 'tp')
- grad_down: float32 [8, 2048, 7168], P('ep', 'tp', 'dp')
- grad_gates: float32 [8, 4096], P('ep', 'dp')
Inputs may be any that keep to these rules, and one draw needn't show every extreme that they name: `expert_ids`: each token names 4 different experts. The 32 tokens of one block name one expert at most 32 times, a bound that some block reaches.
All inputs are finite; a program needn't handle non-finite values.
Results may differ from a plain program's by a relative error of at most 0.02.
Values may be sent and summed in bfloat16 or wider, within the bound.
A program may use at most 64 MiB of HBM per device.

v0:
```python
import jax
import jax.numpy as jnp
from jax import lax
from jax.sharding import PartitionSpec as P


def local(grad_out, expert_ids, gate_values, pre_gate, pre_up, down_weight):
    exp_dev = down_weight.shape[0]
    ep_size = lax.axis_size("ep")
    experts_all = exp_dev * ep_size
    capacity = pre_gate.shape[1] // ep_size
    labels = lax.broadcasted_iota(jnp.int32, (1, 1, experts_all), 2)
    onehot = (expert_ids[:, :, None] == labels).astype(jnp.int32)
    hits = jnp.sum(onehot, axis=1)
    ranks = jnp.cumsum(hits, axis=0) - hits
    slot_rank = jnp.sum(onehot * ranks[:, None, :], axis=2)
    slot_id = expert_ids * capacity + slot_rank
    places = lax.broadcasted_iota(jnp.int32, (experts_all * capacity, 1, 1), 0)
    placing = (slot_id[None, :, :] == places).astype(jnp.bfloat16)
    send_gates = jnp.einsum("jnk,nk->j", placing, gate_values, preferred_element_type=jnp.float32)
    send_gates = send_gates.astype(jnp.bfloat16).reshape(ep_size, exp_dev * capacity)
    selector = jnp.sum(placing, axis=2)
    send_rows = jnp.dot(selector, grad_out, preferred_element_type=jnp.float32).astype(jnp.bfloat16)
    send_rows = send_rows.reshape(ep_size, exp_dev * capacity, send_rows.shape[1])
    got_rows, got_gates = (
        lax.all_to_all(send_rows, "ep", split_axis=0, concat_axis=0, tiled=True),
        lax.all_to_all(send_gates, "ep", split_axis=0, concat_axis=0, tiled=True),
    )
    full_rows = lax.all_gather(got_rows, "tp", axis=2, tiled=True)
    width = full_rows.shape[2]
    rows = (
        full_rows.reshape(ep_size, exp_dev, capacity, width)
        .transpose(1, 0, 2, 3)
        .reshape(exp_dev, ep_size * capacity, width)
    )
    gates = (
        got_gates.reshape(ep_size, exp_dev, capacity)
        .transpose(1, 0, 2)
        .reshape(exp_dev, ep_size * capacity)
        .astype(jnp.float32)
    )
    first = pre_gate.astype(jnp.float32)
    second = pre_up.astype(jnp.float32)
    sigma = jax.nn.sigmoid(first)
    silu_val = first * sigma
    act = (silu_val * second).astype(jnp.bfloat16)
    back = jnp.einsum("erd,ehd->erh", rows, down_weight, preferred_element_type=jnp.float32)
    partial_dots = jnp.sum(back * act.astype(jnp.float32), axis=2)
    grad_gates = lax.psum(partial_dots, "tp")
    grad_act = gates[:, :, None] * back
    grad_pre_gate = (grad_act * second * sigma * (1.0 + first * (1.0 - sigma))).astype(jnp.bfloat16)
    grad_pre_up = (grad_act * silu_val).astype(jnp.bfloat16)
    scaled = (gates[:, :, None] * rows.astype(jnp.float32)).astype(jnp.bfloat16)
    term = jnp.einsum("erh,erd->ehd", act, scaled, preferred_element_type=jnp.float32)
    grad_down = lax.psum_scatter(
        term.astype(jnp.bfloat16), "dp", scatter_dimension=2, tiled=True
    ).astype(jnp.float32)
    return (grad_pre_gate, grad_pre_up, grad_down, grad_gates)


def solution(mesh):
    placed = (
        P(("dp", "ep"), "tp"),
        P(("dp", "ep"), None),
        P(("dp", "ep"), None),
        P("ep", "dp", "tp"),
        P("ep", "dp", "tp"),
        P("ep", "tp", None),
    )
    return jax.shard_map(
        local,
        mesh=mesh,
        in_specs=placed,
        out_specs=(P("ep", "dp", "tp"), P("ep", "dp", "tp"), P("ep", "tp", "dp"), P("ep", "dp")),
        check_vma=False,
    )
```

profile of v0, /device:TPU:1, one launch (start us, length us, event | category | flops | bytes accessed | tf_op | source)
XLA Modules:
  0.0 198.0 jit_solution(14000342814360804535)
XLA Ops:
  7.2 0.0 all-gather.2.cloned.1.call-start
  7.2 0.7 convert_reduce_fusion
  7.9 0.1 copy.32
  8.0 0.1 reduce_window_sum.11
  8.1 0.1 copy.34
  8.1 0.7 select_reduce_fusion
  8.8 0.7 multiply_add_fusion
  9.5 0.1 fusion.20
  9.6 0.3 convolution_convert_fusion.1
  9.9 19.4 %all_to_all.15 = bf16[8,32,896]{2,1,0:T(8,128)(2,1)} all-to-all(bf16[8,32,896]{2,1,0:T(8,128)(2,1)S(1)} %bitcast.42), channel_id=1, replica_groups=mesh['dp'=16,'ep'=8,'tp'=8] {'ep'}, dimensions={0} | all-to-all | bytes 917504 | tf_op jit(solution)/shard_map/all_to_all | solution.py:26
  29.4 0.0 all-gather.2.cloned.1.call-update
  29.4 0.9 fusion.19
  30.3 0.7 all_to_all.12
  31.0 3.3 %all-to-all-start = ((bf16[8,1,32]{2,1,0:T(2,128)(2,1)}), bf16[8,1,32]{2,1,0:T(2,128)(2,1)S(1)}, u32[]{:S(2)}, u32[]{:S(2)}) async-start(bf16[8,1,32]{2,1,0:T(2,128)(2,1)} %all_to_all.12), calls=%async_computation | async-start | bytes 8192 | tf_op jit(solution)/shard_map/all_to_all | solution.py:27
  34.3 0.0 reduce-scatter.4.cloned.1.call-start
  34.3 1.0 copy.37
  35.4 1.0 copy.36
  36.4 4.3 %all-to-all-done = bf16[8,1,32]{2,1,0:T(2,128)(2,1)S(1)} async-done(((bf16[8,1,32]{2,1,0:T(2,128)(2,1)}), bf16[8,1,32]{2,1,0:T(2,128)(2,1)S(1)}, u32[]{:S(2)}, u32[]{:S(2)}) %all-to-all-start) | async-done | bytes 544 | tf_op jit(solution)/shard_map/all_to_all | solution.py:27
  40.7 0.1 reshape.113
  40.8 54.1 %all-gather.2.cloned.1.call-done = bf16[8,32,7168]{2,1,0:T(8,128)(2,1)} async-done(((bf16[8,32,896]{2,1,0:T(8,128)(2,1)}), bf16[8,32,7168]{2,1,0:T(8,128)(2,1)}) %all-gather.2.cloned.1.call-update) | async-done | bytes 3670032 | tf_op jit(solution)/shard_map/all_gather | solution.py:29
  94.9 5.2 %fusion = bf16[1,256,7168]{2,1,0:T(8,128)(2,1)} fusion(bf16[1,256,1,1,1,1,7168]{6,1,5,4,3,2,0:T(8,128)(2,1)} %bitcast.40, f32[256]{0:T(256)S(1)} %reshape.113, bf16[1,256,256]{1,2,0:T(8,128)(2,1)S(1)} %copy.36, bf16[1,256,256]{1,2,0:T(8,128)(2,1)S(1)} %copy.37), kind=kOutput, calls=%fused_computation.1 | convolution fusion | flops 947388416 | bytes 7603200 | tf_op jit(solution)/shard_map/erh,erd->ehd/dot_general | solution.py:54
  100.1 16.3 %copy.42 = bf16[1,256,7168]{1,0,2:T(2,128)(2,1)} copy(bf16[1,256,7168]{2,1,0:T(8,128)(2,1)} %fusion) | data formatting | bytes 7340032
  116.4 5.6 %copy.48 = bf16[7168,1,256]{2,0,1:T(8,128)(2,1)} copy(bf16[7168,1,256]{2,1,0:T(2,128)(2,1)} %bitcast.38) | data formatting | bytes 7340032
  122.0 0.0 reduce-scatter.4.cloned.1.call-update
  122.0 4.4 %fusion.15 = (f32[256]{0:T(256)S(1)}, bf16[1,256,256]{1,2,0:T(8,128)(2,1)S(1)}, bf16[1,256,256]{1,2,0:T(8,128)(2,1)S(1)}) fusion(bf16[1,256,256]{1,2,0:T(8,128)(2,1)S(1)} %copy.36, bf16[1,256,256]{1,2,0:T(8,128)(2,1)S(1)} %copy.37, f32[256]{0:T(256)S(1)} %reshape.113, bf16[256,7168]{1,0:T(8,128)(2,1)} %bitcast.41, bf16[1,256,7168]{2,1,0:T(8,128)(2,1)} %param.11), kind=kOutput, calls=%fused_computation.25 | convolution fusion | flops 940900096 | bytes 7866368 | tf_op jit(solution)/shard_map/erd,ehd->erh/dot_general | solution.py:47
  126.4 0.8 copy.38
  127.2 0.8 copy.39
  127.9 12.5 %psum.7 = f32[1,256]{1,0:T(1,128)} all-reduce(f32[1,256]{1,0:T(1,128)S(1)} %bitcast.43), channel_id=1, replica_groups=mesh['dp'=16,'ep'=8,'tp'=8] {'tp'}, use_global_device_ids=true, to_apply=%region_6.7 | all-reduce | flops 256 | bytes 2048 | tf_op jit(solution)/shard_map/psum | solution.py:49
  140.4 48.0 %reduce-scatter.4.cloned.1.call-done = bf16[448,256]{1,0:T(8,128)(2,1)} async-done(((bf16[7168,256]{1,0:T(8,128)(2,1)}), bf16[448,256]{1,0:T(8,128)(2,1)}) %reduce-scatter.4.cloned.1.call-update) | async-done | bytes 229392
  188.4 1.2 reshape_bitcast_fusion
  189.6 0.6 copy.43
  190.2 0.9 copy.40
  (5 shorter events, 0.0 us)
Async XLA Ops:
  7.2 2.5 %copy-start = (bf16[32,896]{1,0:T(8,128)(2,1)S(1)}, bf16[32,896]{1,0:T(8,128)(2,1)}, u32[]{:S(2)}) copy-start(bf16[32,896]{1,0:T(8,128)(2,1)} %param.6) | copy-start | bytes 172036
  7.2 87.7 %all-gather.2.cloned.1.call-start = ((), (), s32[]{:S(2)}) async-start(), calls=%async_computation.3 | async-start | bytes 4128768 | tf_op jit(solution)/shard_map/all_gather | solution.py:29
  31.0 9.7 %all-to-all-start = ((bf16[8,1,32]{2,1,0:T(2,128)(2,1)}), bf16[8,1,32]{2,1,0:T(2,128)(2,1)S(1)}, u32[]{:S(2)}, u32[]{:S(2)}) async-start(bf16[8,1,32]{2,1,0:T(2,128)(2,1)} %all_to_all.12), calls=%async_computation | async-start | bytes 8192 | tf_op jit(solution)/shard_map/all_to_all | solution.py:27
  34.3 154.1 %reduce-scatter.4.cloned.1.call-start = ((), (), s32[]{:S(2)}) async-start(), calls=%async_computation.4 | async-start | bytes 3899392
Sparse Core Ops, SparseCore 0:
  29.5 65.2 all-gather.1
  122.2 66.2 reduce-scatter.3
where the time goes:
time: 201 us; the launch traced here: 198 us
  waiting for transfers between devices  106 us (53%)
  blocking collectives  31.9 us (16%)
  local copies, waits for them, and re-layouts  29.1 us (14%)
  between operations  14.1 us (7%)
  matrix products  10.8 us (5%)
  starting transfers between devices  3.39 us (2%)
  other arithmetic  2.25 us (1%)
    all_gather x1, waiting for transfers between devices, local(): full_rows = lax.all_gather(got_rows, 'tp', axis=2, tiled=True)  54.1 us
    unnamed x3, waiting for transfers between devices  48 us
    unnamed x11, local copies, waits for them, and re-layouts  28.2 us
    all_to_all x1, blocking collectives, local(): lax.all_to_all(send_rows, 'ep', split_axis=0, concat_axis=0, tiled=True)  19.4 us
    psum x1, blocking collectives, local(): grad_gates = lax.psum(partial_dots, 'tp')  12.5 us
    dot_general x1, matrix products, local(): jnp.einsum('erh,erd->ehd', act, scaled, preferred_element_type=jnp.float32)  5.23 us
    dot_general x1, matrix products, local(): jnp.einsum('erd,ehd->erh', rows, down_weight, preferred_element_type=jnp....  4.37 us
    all_to_all x1, waiting for transfers between devices, local(): lax.all_to_all(send_gates, 'ep', split_axis=0, concat_axis=0, tiled=True)  4.3 us
  transfers between devices with their start and end apart: 3, of which 3 were waited for; matrix products, arithmetic and copies ran while one was open for 4% of the time, Pallas kernels for 0%

commit v1 on v0

v1 whole, which is shorter than its diff:
```python
import functools

import jax
import jax.numpy as jnp
from jax import lax
from jax.experimental import pallas as pl
from jax.experimental.pallas import tpu as pltpu
from jax.sharding import PartitionSpec as P

MESH = pl.DeviceIdType.MESH
F32 = jnp.float32
BF16 = jnp.bfloat16
LANE = 128
STAGES = 4
ROWS = ((0, 32), (32, 32), (64, 32), (96, 16))
SLAB = 112


def dot(a, b, dims=((1,), (0,))):
    return lax.dot_general(a, b, (dims, ((), ())), preferred_element_type=F32)


def kernel(
    nx, ny, nz,
    grad_ref, ids_ref, gate_ref, pg_hbm, pu_hbm, w_hbm,
    dpg_ref, dpu_ref, down_ref, dgate_ref,
    ta, tb, meta, w, pg, pu, act, st, sm, at, am, gslot, back,
    own, away, mate, own3, away3, mate3,
    out_r, in_r, out_3, in_3, dots,
    sem_local, p1_send, p1_recv, meta_send, meta_recv,
    ag_send, ag_recv, mate_send, mate_recv, rs_send, rs_recv, dot_send, dot_recv,
):
    tok = grad_ref.shape[0]
    rows = ny * tok
    hidden = pg.shape[1]
    x, y, dp = lax.axis_index("tp"), lax.axis_index("ep"), lax.axis_index("dp")
    z, core = dp // 2, dp % 2
    kx, ky, kz = nx // 2, ny // 2, nz // 2
    assert kx == nx // 2 and nx == nz

    def at_x(d):
        return {"tp": lax.rem(x + d + nx, nx)}

    def at_y(d):
        return {"ep": lax.rem(y + d + ny, ny)}

    def at_z(d):
        return {"dp": lax.rem(z + d + nz, nz) * 2 + core}

    other = {"dp": z * 2 + 1 - core}

    barrier = pltpu.get_barrier_semaphore()
    peers = [at_x(k) for k in range(1, nx)] + [at_y(k) for k in range(1, ny)] + [other]
    peers += [at_z(1), at_z(-1)]
    for peer in peers:
        pl.semaphore_signal(barrier, inc=1, device_id=peer, device_id_type=MESH)

    locals_ = [
        pltpu.make_async_copy(pg_hbm.at[0], pg, sem_local.at[0]),
        pltpu.make_async_copy(pu_hbm.at[0], pu, sem_local.at[1]),
        pltpu.make_async_copy(w_hbm.at[0], w, sem_local.at[2]),
    ]
    for c in locals_:
        c.start()

    for s in range(3):
        ta[x, y, 32 * s:32 * s + 32, :] = grad_ref[:, LANE * s:LANE * (s + 1)]
        tb[x, y, 32 * s:32 * s + 32, :] = grad_ref[:, LANE * (s + 4):LANE * (s + 5)]
    ta[x, y, 96:112, :] = grad_ref[0:16, 3 * LANE:4 * LANE]
    tb[x, y, 96:112, :] = grad_ref[16:32, 3 * LANE:4 * LANE]
    lanes = lax.broadcasted_iota(jnp.int32, (tok, LANE), 1)
    table = jnp.zeros((tok, LANE), F32)
    gates = gate_ref[...].astype(F32)
    for k in range(ids_ref.shape[1]):
        named = ids_ref[:, k:k + 1]
        table = jnp.where(lanes == named, gates[:, k:k + 1], table)
        table = jnp.where(lanes == named + 64, 1.0, table)
    meta[y] = table.astype(BF16)

    pl.semaphore_wait(barrier, len(peers))

    def p1(path, part, k):
        lo, n = (0, 32) if part == 0 else (32, SLAB - 32)
        buf = ta if path == 0 else tb
        ref = buf.at[x, y, pl.ds(lo, n), :]
        return pltpu.make_async_remote_copy(
            src_ref=ref, dst_ref=ref,
            send_sem=p1_send.at[path, part, k], recv_sem=p1_recv.at[path, part, k],
            device_id=at_y(k) if path == 0 else at_x(k), device_id_type=MESH,
        )

    def meta_copy(k):
        return pltpu.make_async_remote_copy(
            src_ref=meta.at[y], dst_ref=meta.at[y],
            send_sem=meta_send.at[k], recv_sem=meta_recv.at[k],
            device_id=at_y(k), device_id_type=MESH,
        )

    p1_all = [(0, k) for k in range(1, ny)] + [(1, k) for k in range(1, nx)]
    for path, k in p1_all:
        p1(path, 0, k).start()
    for k in range(1, ny):
        meta_copy(k).start()
    for path, k in p1_all:
        p1(path, 1, k).start()

    def ag(s, k, path, right):
        lo, n = ROWS[s]
        last = k == (kx if path == 0 else ky) - 1
        step = -k if right else k
        if path == 0:
            half = ny // 2
            span = pl.ds(0 if right else half, half) if last else pl.ds(0, ny)
            ref = ta.at[lax.rem(x + step + nx, nx), span, pl.ds(lo, n), :]
            to = at_x(1 if right else -1)
        else:
            half = nx // 2
            span = pl.ds(0 if right else half, half) if last else pl.ds(0, nx)
            ref = tb.at[span, lax.rem(y + step + ny, ny), pl.ds(lo, n), :]
            to = at_y(1 if right else -1)
        return pltpu.make_async_remote_copy(
            src_ref=ref, dst_ref=ref,
            send_sem=ag_send.at[s, k, path, int(right)],
            recv_sem=ag_recv.at[s, k, path, int(right)],
            device_id=to, device_id_type=MESH,
        )

    steps = max(kx, ky)

    def streams(k):
        return [(p, r) for p in (0, 1) for r in (True, False) if k < (kx if p == 0 else ky)]

    def ag_start(s, k):
        for p, r in streams(k):
            if k > 0:
                ag(s, k - 1, p, r).wait_recv()
            ag(s, k, p, r).start()

    def ag_finish(s):
        for p in (0, 1):
            for r in (True, False):
                ag(s, (kx if p == 0 else ky) - 1, p, r).wait_recv()

    def prepare():
        locals_[0].wait()
        locals_[1].wait()
        gate_pre = pg[...].astype(F32)
        up_pre = pu[...].astype(F32)
        sigma = jax.nn.sigmoid(gate_pre)
        act[...] = (gate_pre * sigma * up_pre).astype(BF16)
        for k in range(1, ny):
            meta_copy(k).wait_recv()
        tables = meta[...].reshape(rows, LANE)
        tables32 = tables.astype(F32)
        at_row = lax.broadcasted_iota(jnp.int32, (rows, rows), 0)
        at_col = lax.broadcasted_iota(jnp.int32, (rows, rows), 1)
        before = (at_row // tok == at_col // tok) & (at_col < at_row)
        before = jnp.where(before, 1.0, 0.0).astype(BF16)
        ranks = dot(before, tables)
        lane = lax.broadcasted_iota(jnp.int32, (rows, LANE), 1)
        gate_t = jnp.sum(jnp.where(lane == y, tables32, 0.0), axis=1, keepdims=True)
        member = jnp.sum(jnp.where(lane == y + 64, tables32, 0.0), axis=1, keepdims=True)
        rank = jnp.sum(jnp.where(lane == y + 64, ranks, 0.0), axis=1, keepdims=True)
        slot = rank.astype(jnp.int32) + at_row[:, 0:1] // tok * tok
        place = jnp.where(at_col == slot, member, 0.0)
        sm32 = place.T
        sm[...] = sm32.astype(BF16)
        gslot[...] = jnp.sum(
            jnp.where(lane == y, dot(sm[...], tables), 0.0), axis=1, keepdims=True
        )
        moved = dot(place.astype(BF16), act[...]) * gate_t
        am[...] = moved.astype(BF16)
        at[...] = moved.T.astype(BF16)
        back[...] = jnp.zeros_like(back)

    def compute(s):
        if s < 3:
            def body(i, carry):
                lo = ROWS[s][0]
                left = ta[i, :, lo:lo + 32, :].reshape(rows, LANE)
                right = tb[i, :, lo:lo + 32, :].reshape(rows, LANE)
                both = jnp.concatenate([left, right], axis=1)
                first = pl.multiple_of(i * 7 * LANE + s * LANE, LANE)
                second = pl.multiple_of(i * 7 * LANE + (s + 4) * LANE, LANE)
                wide = jnp.concatenate(
                    [w[:, pl.ds(first, LANE)], w[:, pl.ds(second, LANE)]], axis=1
                )
                term = dot(at[...], both)
                mine = jnp.where(core == 0, term[:, :LANE], term[:, LANE:])
                theirs = jnp.where(core == 0, term[:, LANE:], term[:, :LANE])
                own[s, i] = mine
                away[s, i] = theirs.astype(BF16)
                back[...] += dot(both, wide, ((1,), (1,)))
                return carry
        else:
            def body(i, carry):
                lo = ROWS[s][0]
                top = ta[i, :, lo:lo + 16, :]
                low = tb[i, :, lo:lo + 16, :]
                tile = jnp.concatenate([top, low], axis=1).reshape(rows, LANE)
                first = pl.multiple_of(i * 7 * LANE + 3 * LANE, LANE)
                term = dot(tile, am[...], ((0,), (0,)))
                half = LANE // 2
                mine = jnp.where(core == 0, term[:half], term[half:])
                theirs = jnp.where(core == 0, term[half:], term[:half])
                own3[i] = mine
                away3[i] = theirs.astype(BF16)
                back[...] += dot(tile, w[:, pl.ds(first, LANE)], ((1,), (1,)))
                return carry
        lax.fori_loop(0, nx, body, 0)

    def swap(s):
        return pltpu.make_async_remote_copy(
            src_ref=away.at[s] if s < 3 else away3,
            dst_ref=mate.at[s] if s < 3 else mate3,
            send_sem=mate_send.at[s], recv_sem=mate_recv.at[s],
            device_id=other, device_id_type=MESH,
        )

    def rs(s, r, right):
        size = hidden if s < 3 else LANE // 2
        half = size // 2
        if r == 0:
            span = pl.ds(0 if right else half, half)
        else:
            span = pl.ds(0, size)
        d = int(right)
        if s < 3:
            src, dst = out_r.at[s, r, d, span, :], in_r.at[s, r, d, span, :]
        else:
            src, dst = out_3.at[r, d, span, :], in_3.at[r, d, span, :]
        return pltpu.make_async_remote_copy(
            src_ref=src, dst_ref=dst,
            send_sem=rs_send.at[s, r, d], recv_sem=rs_recv.at[s, r, d],
            device_id=at_z(1 if right else -1), device_id_type=MESH,
        )

    def chip_sum(s, o, lo, n):
        if s < 3:
            return own[s, o, lo:lo + n, :] + mate[s, o, lo:lo + n, :].astype(F32)
        return own3[o, lo:lo + n, :] + mate3[o, lo:lo + n, :].astype(F32)

    def came(s, r, d, lo, n):
        if s < 3:
            return in_r[s, r, d, lo:lo + n, :].astype(F32)
        return in_3[r, d, lo:lo + n, :].astype(F32)

    def rs_start(s, r):
        size = hidden if s < 3 else LANE // 2
        half = size // 2
        if r == 0:
            swap(s).wait_recv()
        for right in (True, False):
            d = int(right)
            o = lax.rem(z + (kz - r if right else r - kz) + nz, nz)
            if r > 0:
                rs(s, r - 1, right).wait_recv()
            for lo in (0, half):
                in_half = (lo == 0) == right
                if r == 0 and not in_half:
                    continue
                value = chip_sum(s, o, lo, half)
                if r > 1 or (r == 1 and in_half):
                    value = value + came(s, r - 1, d, lo, half)
                if s < 3:
                    out_r[s, r, d, lo:lo + half, :] = value.astype(BF16)
                else:
                    out_3[r, d, lo:lo + half, :] = value.astype(BF16)
            rs(s, r, right).start()

    def rs_finish(s):
        size = hidden if s < 3 else LANE // 2
        half = size // 2
        for right in (True, False):
            rs(s, kz - 1, right).wait_recv()
        parts = []
        for lo in (0, half):
            value = chip_sum(s, z, lo, half)
            for d in (1, 0):
                if kz > 1 or (lo == 0) == (d == 1):
                    value = value + came(s, kz - 1, d, lo, half)
            parts.append(value)
        value = jnp.concatenate(parts, axis=0)
        if s < 3:
            @pl.when(core == 0)
            def _():
                down_ref[0, :, LANE * s:LANE * (s + 1)] = value

            @pl.when(core == 1)
            def _():
                down_ref[0, :, LANE // 2 + LANE * s:LANE // 2 + LANE * (s + 1)] = value
        else:
            turned = value.T

            @pl.when(core == 0)
            def _():
                down_ref[0, :, 3 * LANE:3 * LANE + LANE // 2] = turned

            @pl.when(core == 1)
            def _():
                down_ref[0, :, 0:LANE // 2] = turned

    def dot_copy(k):
        return pltpu.make_async_remote_copy(
            src_ref=dots.at[x], dst_ref=dots.at[x],
            send_sem=dot_send.at[k], recv_sem=dot_recv.at[k],
            device_id=at_x(k), device_id_type=MESH,
        )

    def finish_slots():
        whole = back[...]
        high = whole.astype(BF16)
        low = (whole - high.astype(F32)).astype(BF16)
        placed = dot(sm[...], high) + dot(sm[...], low)
        prod = placed * act[...].astype(F32)
        total = jnp.sum(prod.T, axis=0, keepdims=True)
        dots[x] = jnp.broadcast_to(total, (8, rows))
        for k in range(1, nx):
            dot_copy(k).start()
        gate_pre = pg[...].astype(F32)
        up_pre = pu[...].astype(F32)
        sigma = jax.nn.sigmoid(gate_pre)
        grad_act = gslot[...] * placed
        dpg_ref[0] = (grad_act * up_pre * sigma * (1.0 + gate_pre * (1.0 - sigma))).astype(BF16)
        dpu_ref[0] = (grad_act * (gate_pre * sigma)).astype(BF16)

    def finish_dots():
        for k in range(1, nx):
            dot_copy(k).wait_recv()
        total = dots[0]
        for i in range(1, nx):
            total = total + dots[i]
        dgate_ref[...] = total[0:1, :]

    def p1_wait(part):
        for path, k in p1_all:
            p1(path, part, k).wait_recv()

    for t in range(2 * STAGES + steps + kz + 2):
        for s in range(STAGES):
            k = t - 2 * s
            if 0 <= k < steps:
                if s <= 1 and k == 0:
                    p1_wait(s)
                ag_start(s, k)
            if k == steps:
                ag_finish(s)
            r = k - steps - 1
            if 0 <= r < kz:
                rs_start(s, r)
            if r == kz:
                rs_finish(s)
        if t == 0:
            prepare()
            locals_[2].wait()
        for s in range(STAGES):
            if t - 2 * s == steps:
                compute(s)
                swap(s).start()
                if s == STAGES - 1:
                    finish_slots()
    finish_dots()

    for path, k in p1_all:
        for part in (0, 1):
            p1(path, part, k).wait_send()
    for k in range(1, ny):
        meta_copy(k).wait_send()
    for s in range(STAGES):
        for k in range(steps):
            for p, r in streams(k):
                ag(s, k, p, r).wait_send()
        swap(s).wait_send()
        for r in range(kz):
            for right in (True, False):
                rs(s, r, right).wait_send()
    for k in range(1, nx):
        dot_copy(k).wait_send()


def solution(mesh):
    nx, ny, nz = mesh.shape["tp"], mesh.shape["ep"], mesh.shape["dp"] // 2
    steps = max(nx, ny) // 2

    def local(grad_out, expert_ids, gate_values, pre_gate, pre_up, down_weight):
        rows, hidden = pre_gate.shape[1:]
        width = down_weight.shape[2]
        tok = grad_out.shape[0]
        half = LANE // 2
        kz = nz // 2
        dma = pltpu.SemaphoreType.DMA
        vmem = pl.BlockSpec(memory_space=pltpu.VMEM)
        hbm = pl.BlockSpec(memory_space=pl.ANY)
        return pl.pallas_call(
            functools.partial(kernel, nx, ny, nz),
            out_shape=(
                jax.ShapeDtypeStruct(pre_gate.shape, BF16),
                jax.ShapeDtypeStruct(pre_up.shape, BF16),
                jax.ShapeDtypeStruct((1, hidden, width // (2 * nz)), F32),
                jax.ShapeDtypeStruct((1, rows), F32),
            ),
            in_specs=[vmem, vmem, vmem, hbm, hbm, hbm],
            out_specs=(vmem, vmem, vmem, vmem),
            scratch_shapes=[
                pltpu.VMEM((nx, ny, SLAB, LANE), BF16),
                pltpu.VMEM((nx, ny, SLAB, LANE), BF16),
                pltpu.VMEM((ny, tok, LANE), BF16),
                pltpu.VMEM((hidden, width), BF16),
                pltpu.VMEM((rows, hidden), BF16),
                pltpu.VMEM((rows, hidden), BF16),
                pltpu.VMEM((rows, hidden), BF16),
                pltpu.VMEM((rows, rows), BF16),
                pltpu.VMEM((rows, rows), BF16),
                pltpu.VMEM((hidden, rows), BF16),
                pltpu.VMEM((rows, hidden), BF16),
                pltpu.VMEM((rows, 1), F32),
                pltpu.VMEM((rows, hidden), F32),
                pltpu.VMEM((3, nx, hidden, LANE), F32),
                pltpu.VMEM((3, nx, hidden, LANE), BF16),
                pltpu.VMEM((3, nx, hidden, LANE), BF16),
                pltpu.VMEM((nx, half, hidden), F32),
                pltpu.VMEM((nx, half, hidden), BF16),
                pltpu.VMEM((nx, half, hidden), BF16),
                pltpu.VMEM((3, kz, 2, hidden, LANE), BF16),
                pltpu.VMEM((3, kz, 2, hidden, LANE), BF16),
                pltpu.VMEM((kz, 2, half, hidden), BF16),
                pltpu.VMEM((kz, 2, half, hidden), BF16),
                pltpu.VMEM((nx, 8, rows), F32),
                dma((3,)),
                dma((2, 2, max(nx, ny))),
                dma((2, 2, max(nx, ny))),
                dma((ny,)),
                dma((ny,)),
                dma((STAGES, steps, 2, 2)),
                dma((STAGES, steps, 2, 2)),
                dma((STAGES,)),
                dma((STAGES,)),
                dma((STAGES, kz, 2)),
                dma((STAGES, kz, 2)),
                dma((nx,)),
                dma((nx,)),
            ],
            compiler_params=pltpu.CompilerParams(
                collective_id=0, has_side_effects=True, vmem_limit_bytes=48 * 1024 * 1024
            ),
        )(grad_out, expert_ids, gate_values, pre_gate, pre_up, down_weight)

    placed = (
        P(("dp", "ep"), "tp"),
        P(("dp", "ep"), None),
        P(("dp", "ep"), None),
        P("ep", "dp", "tp"),
        P("ep", "dp", "tp"),
        P("ep", "tp", None),
    )
    return jax.shard_map(
        local,
        mesh=mesh,
        in_specs=placed,
        out_specs=(P("ep", "dp", "tp"), P("ep", "dp", "tp"), P("ep", "tp", "dp"), P("ep", "dp")),
        check_vma=False,
    )
```

time: 201 us -> 99.5 us (0.50)
  the two profiles are of different devices: /device:TPU:1 before, /device:TPU:2 now
where the time goes in v1:
time: 99.5 us; the launch traced here: 99.2 us
  Pallas kernels  89.5 us (90%)
  local copies, waits for them, and re-layouts  9.03 us (9%)
    pallas_call x1, Pallas kernels, local(): pl.pallas_call(functools.partial(kernel, nx, ny, nz), out_shape=(jax.Shap...  89.5 us
    unnamed x13, local copies, waits for them, and re-layouts  8.07 us

profile of v1, /device:TPU:2, one launch (start us, length us, event | category | flops | bytes accessed | tf_op | source)
XLA Modules:
  0.0 99.2 jit_solution(13487434105908197025)
XLA Ops:
  0.6 0.8 copy.11.gate_ref
  1.4 0.8 copy.10.ids_ref
  2.2 0.0 copy-start
  2.2 2.0 %copy-done = bf16[1,256,7168]{2,1,0:T(8,128)(2,1)S(1)} copy-done((bf16[1,256,7168]{2,1,0:T(8,128)(2,1)S(1)}, bf16[1,256,7168]{2,1,0:T(8,128)(2,1)}, u32[]{:S(2)}) %copy-start) | copy-done | bytes 3670040
  4.2 0.0 copy-start.1
  4.2 0.9 copy-done.1
  5.1 0.0 copy-start.2
  5.1 0.9 copy-done.2
  6.0 0.0 copy-start.3
  6.0 0.8 copy-done.3
  6.8 89.5 %shard_map.93 = (bf16[1,256,256]{2,1,0:T(8,128)(2,1)S(1)}, bf16[1,256,256]{2,1,0:T(8,128)(2,1)S(1)}, f32[1,256,448]{2,1,0:T(8,128)S(1)}, f32[1,256]{1,0:T(1,128)S(1)}) custom-call(bf16[32,896]{1,0:T(8,128)(2,1)S(1)} %copy-done.3, s32[32,4]{1,0:T(8,128)S(1)} %copy.10.ids_ref, bf16[32,4]{1,0:T(8,128)(2,1)S(1)} %copy.11.gate_ref, ...), custom_call_target="tpu_custom_call" | custom-call | tf_op jit(solution)/shard_map/pallas_call | solution.py:394
  96.3 1.0 copy.12
  97.3 0.7 copy.16
  98.0 0.7 copy.17
  98.6 0.6 copy.18
Async XLA Ops:
  2.2 2.0 %copy-start = (bf16[1,256,7168]{2,1,0:T(8,128)(2,1)S(1)}, bf16[1,256,7168]{2,1,0:T(8,128)(2,1)}, u32[]{:S(2)}) copy-start(bf16[1,256,7168]{2,1,0:T(8,128)(2,1)} %w_hbm.1) | copy-start | bytes 11010052
  4.2 0.9 copy-start.1
  5.1 0.9 copy-start.2
  6.0 0.8 copy-start.3

commit v2 on v1

--- a/solution.py
+++ b/solution.py
@@ -22,12 +22,13 @@
 
 def kernel(
     nx, ny, nz,
-    grad_ref, ids_ref, gate_ref, pg_hbm, pu_hbm, w_hbm,
-    dpg_ref, dpu_ref, down_ref, dgate_ref,
-    ta, tb, meta, w, pg, pu, act, st, sm, at, am, gslot, back,
+    grad_hbm, ids_hbm, gate_hbm, pg_hbm, pu_hbm, w_hbm,
+    dpg_hbm, dpu_hbm, down_hbm, dgate_ref,
+    grad_ref, ids_ref, gate_ref,
+    ta, tb, meta, w, pg, pu, act, sm, at, am, gslot, back,
     own, away, mate, own3, away3, mate3,
-    out_r, in_r, out_3, in_3, dots,
-    sem_local, p1_send, p1_recv, meta_send, meta_recv,
+    out_r, in_r, out_3, in_3, dots, dpg_ref, dpu_ref, down_ref,
+    sem_local, sem_out, p1_send, p1_recv, meta_send, meta_recv,
     ag_send, ag_recv, mate_send, mate_recv, rs_send, rs_recv, dot_send, dot_recv,
 ):
     tok = grad_ref.shape[0]
@@ -55,6 +56,13 @@
     for peer in peers:
         pl.semaphore_signal(barrier, inc=1, device_id=peer, device_id_type=MESH)
 
+    first = [
+        pltpu.make_async_copy(grad_hbm, grad_ref, sem_local.at[3]),
+        pltpu.make_async_copy(ids_hbm, ids_ref, sem_local.at[4]),
+        pltpu.make_async_copy(gate_hbm, gate_ref, sem_local.at[5]),
+    ]
+    for c in first:
+        c.start()
     locals_ = [
         pltpu.make_async_copy(pg_hbm.at[0], pg, sem_local.at[0]),
         pltpu.make_async_copy(pu_hbm.at[0], pu, sem_local.at[1]),
@@ -63,19 +71,21 @@
     for c in locals_:
         c.start()
 
+    for c in first:
+        c.wait()
     for s in range(3):
         ta[x, y, 32 * s:32 * s + 32, :] = grad_ref[:, LANE * s:LANE * (s + 1)]
         tb[x, y, 32 * s:32 * s + 32, :] = grad_ref[:, LANE * (s + 4):LANE * (s + 5)]
     ta[x, y, 96:112, :] = grad_ref[0:16, 3 * LANE:4 * LANE]
     tb[x, y, 96:112, :] = grad_ref[16:32, 3 * LANE:4 * LANE]
-    lanes = lax.broadcasted_iota(jnp.int32, (tok, LANE), 1)
-    table = jnp.zeros((tok, LANE), F32)
+    labels = lax.broadcasted_iota(jnp.int32, (LANE, tok), 0)
+    table = jnp.zeros((LANE, tok), F32)
     gates = gate_ref[...].astype(F32)
-    for k in range(ids_ref.shape[1]):
-        named = ids_ref[:, k:k + 1]
-        table = jnp.where(lanes == named, gates[:, k:k + 1], table)
-        table = jnp.where(lanes == named + 64, 1.0, table)
-    meta[y] = table.astype(BF16)
+    for k in range(ids_ref.shape[0]):
+        named = ids_ref[k:k + 1, :]
+        table = jnp.where(labels == named, gates[k:k + 1, :], table)
+        table = jnp.where(labels == named + 64, 1.0, table)
+    meta[y] = table.T.astype(BF16)
 
     pl.semaphore_wait(barrier, len(peers))
 
@@ -97,6 +107,7 @@
         )
 
     p1_all = [(0, k) for k in range(1, ny)] + [(1, k) for k in range(1, nx)]
+    p1_all.sort(key=lambda e: abs(e[1] - (ny if e[0] == 0 else nx) // 2))
     for path, k in p1_all:
         p1(path, 0, k).start()
     for k in range(1, ny):
@@ -173,47 +184,61 @@
         at[...] = moved.T.astype(BF16)
         back[...] = jnp.zeros_like(back)
 
-    def compute(s):
+    def owner(i):
+        return lax.rem(z + lax.select(i % 2 == 1, kz - (i + 1) // 2, i // 2 - kz) + nz, nz)
+
+    def columns(s, i):
+        lo, n = ROWS[s]
+        a_part, b_part = ta[i, :, lo:lo + n, :], tb[i, :, lo:lo + n, :]
         if s < 3:
-            def body(i, carry):
-                lo = ROWS[s][0]
-                left = ta[i, :, lo:lo + 32, :].reshape(rows, LANE)
-                right = tb[i, :, lo:lo + 32, :].reshape(rows, LANE)
-                both = jnp.concatenate([left, right], axis=1)
-                first = pl.multiple_of(i * 7 * LANE + s * LANE, LANE)
-                second = pl.multiple_of(i * 7 * LANE + (s + 4) * LANE, LANE)
-                wide = jnp.concatenate(
-                    [w[:, pl.ds(first, LANE)], w[:, pl.ds(second, LANE)]], axis=1
-                )
-                term = dot(at[...], both)
-                mine = jnp.where(core == 0, term[:, :LANE], term[:, LANE:])
-                theirs = jnp.where(core == 0, term[:, LANE:], term[:, :LANE])
+            return jnp.concatenate(
+                [a_part.reshape(rows, LANE), b_part.reshape(rows, LANE)], axis=1
+            )
+        return jnp.concatenate([a_part, b_part], axis=1).reshape(rows, LANE)
+
+    def terms(s, lo, hi):
+        half = LANE // 2
+
+        def body(i, carry):
+            block = columns(s, owner(i))
+            if s < 3:
+                term = dot(at[...], block)
+                first, second = term[:, :LANE], term[:, LANE:]
+            else:
+                term = dot(block, am[...], ((0,), (0,)))
+                first, second = term[:half], term[half:]
+            mine = jnp.where(core == 0, first, second)
+            theirs = jnp.where(core == 0, second, first).astype(BF16)
+            if s < 3:
                 own[s, i] = mine
-                away[s, i] = theirs.astype(BF16)
-                back[...] += dot(both, wide, ((1,), (1,)))
-                return carry
-        else:
-            def body(i, carry):
-                lo = ROWS[s][0]
-                top = ta[i, :, lo:lo + 16, :]
-                low = tb[i, :, lo:lo + 16, :]
-                tile = jnp.concatenate([top, low], axis=1).reshape(rows, LANE)
-                first = pl.multiple_of(i * 7 * LANE + 3 * LANE, LANE)
-                term = dot(tile, am[...], ((0,), (0,)))
-                half = LANE // 2
-                mine = jnp.where(core == 0, term[:half], term[half:])
-                theirs = jnp.where(core == 0, term[half:], term[:half])
+                away[s, i] = theirs
+            else:
                 own3[i] = mine
-                away3[i] = theirs.astype(BF16)
-                back[...] += dot(tile, w[:, pl.ds(first, LANE)], ((1,), (1,)))
-                return carry
+                away3[i] = theirs
+            return carry
+        lax.fori_loop(lo, hi, body, 0)
+
+    def backs(s):
+        def body(i, carry):
+            block = columns(s, i)
+            base = i * 7 * LANE
+            first = pl.multiple_of(base + s * LANE, LANE)
+            weights = w[:, pl.ds(first, LANE)]
+            if s < 3:
+                second = pl.multiple_of(base + (s + 4) * LANE, LANE)
+                weights = jnp.concatenate([weights, w[:, pl.ds(second, LANE)]], axis=1)
+            back[...] += dot(block, weights, ((1,), (1,)))
+            return carry
         lax.fori_loop(0, nx, body, 0)
 
-    def swap(s):
+    cut = min(3, nx - 1)
+
+    def swap(s, part):
+        span = pl.ds(0, cut) if part == 0 else pl.ds(cut, nx - cut)
+        src, dst = (away.at[s], mate.at[s]) if s < 3 else (away3, mate3)
         return pltpu.make_async_remote_copy(
-            src_ref=away.at[s] if s < 3 else away3,
-            dst_ref=mate.at[s] if s < 3 else mate3,
-            send_sem=mate_send.at[s], recv_sem=mate_recv.at[s],
+            src_ref=src.at[span], dst_ref=dst.at[span],
+            send_sem=mate_send.at[s, part], recv_sem=mate_recv.at[s, part],
             device_id=other, device_id_type=MESH,
         )
 
@@ -235,10 +260,10 @@
             device_id=at_z(1 if right else -1), device_id_type=MESH,
         )
 
-    def chip_sum(s, o, lo, n):
+    def chip_sum(s, i, lo, n):
         if s < 3:
-            return own[s, o, lo:lo + n, :] + mate[s, o, lo:lo + n, :].astype(F32)
-        return own3[o, lo:lo + n, :] + mate3[o, lo:lo + n, :].astype(F32)
+            return own[s, i, lo:lo + n, :] + mate[s, i, lo:lo + n, :].astype(F32)
+        return own3[i, lo:lo + n, :] + mate3[i, lo:lo + n, :].astype(F32)
 
     def came(s, r, d, lo, n):
         if s < 3:
@@ -248,18 +273,18 @@
     def rs_start(s, r):
         size = hidden if s < 3 else LANE // 2
         half = size // 2
-        if r == 0:
-            swap(s).wait_recv()
+        if r in (0, 2):
+            swap(s, r // 2).wait_recv()
         for right in (True, False):
             d = int(right)
-            o = lax.rem(z + (kz - r if right else r - kz) + nz, nz)
+            chunk = max(2 * r - d, 0)
             if r > 0:
                 rs(s, r - 1, right).wait_recv()
             for lo in (0, half):
                 in_half = (lo == 0) == right
                 if r == 0 and not in_half:
                     continue
-                value = chip_sum(s, o, lo, half)
+                value = chip_sum(s, chunk, lo, half)
                 if r > 1 or (r == 1 and in_half):
                     value = value + came(s, r - 1, d, lo, half)
                 if s < 3:
@@ -271,34 +296,38 @@
     def rs_finish(s):
         size = hidden if s < 3 else LANE // 2
         half = size // 2
+        if kz <= 2:
+            swap(s, 1).wait_recv()
         for right in (True, False):
             rs(s, kz - 1, right).wait_recv()
         parts = []
         for lo in (0, half):
-            value = chip_sum(s, z, lo, half)
+            value = chip_sum(s, nz - 1, lo, half)
             for d in (1, 0):
                 if kz > 1 or (lo == 0) == (d == 1):
                     value = value + came(s, kz - 1, d, lo, half)
             parts.append(value)
         value = jnp.concatenate(parts, axis=0)
         if s < 3:
-            @pl.when(core == 0)
-            def _():
-                down_ref[0, :, LANE * s:LANE * (s + 1)] = value
-
-            @pl.when(core == 1)
-            def _():
-                down_ref[0, :, LANE // 2 + LANE * s:LANE // 2 + LANE * (s + 1)] = value
+            down_ref[s] = value.T
+            down_copy(s).start()
         else:
-            turned = value.T
-
-            @pl.when(core == 0)
-            def _():
-                down_ref[0, :, 3 * LANE:3 * LANE + LANE // 2] = turned
-
-            @pl.when(core == 1)
-            def _():
-                down_ref[0, :, 0:LANE // 2] = turned
+            down_ref[s, 0:LANE // 2, :] = value
+            down_copy(s).start()
+
+    def down_copy(s):
+        first = LANE * s + core * (LANE // 2) if s < 3 else (1 - core) * 3 * LANE
+        size = LANE if s < 3 else LANE // 2
+        return pltpu.make_async_copy(
+            down_ref.at[s, pl.ds(0, size), :],
+            down_hbm.at[0, pl.ds(pl.multiple_of(first, 8), size), :],
+            sem_out.at[s],
+        )
+
+    slot_copies = [
+        pltpu.make_async_copy(dpg_ref, dpg_hbm.at[0], sem_out.at[4]),
+        pltpu.make_async_copy(dpu_ref, dpu_hbm.at[0], sem_out.at[5]),
+    ]
 
     def dot_copy(k):
         return pltpu.make_async_remote_copy(
@@ -321,8 +350,10 @@
         up_pre = pu[...].astype(F32)
         sigma = jax.nn.sigmoid(gate_pre)
         grad_act = gslot[...] * placed
-        dpg_ref[0] = (grad_act * up_pre * sigma * (1.0 + gate_pre * (1.0 - sigma))).astype(BF16)
-        dpu_ref[0] = (grad_act * (gate_pre * sigma)).astype(BF16)
+        dpg_ref[...] = (grad_act * up_pre * sigma * (1.0 + gate_pre * (1.0 - sigma))).astype(BF16)
+        dpu_ref[...] = (grad_act * (gate_pre * sigma)).astype(BF16)
+        for c in slot_copies:
+            c.start()
 
     def finish_dots():
         for k in range(1, nx):
@@ -332,33 +363,38 @@
             total = total + dots[i]
         dgate_ref[...] = total[0:1, :]
 
+    def multiply(s):
+        ag_finish(s)
+        if s == 0:
+            locals_[2].wait()
+        terms(s, 0, cut)
+        swap(s, 0).start()
+        terms(s, cut, nx)
+        swap(s, 1).start()
+
     def p1_wait(part):
         for path, k in p1_all:
             p1(path, part, k).wait_recv()
 
-    for t in range(2 * STAGES + steps + kz + 2):
-        for s in range(STAGES):
-            k = t - 2 * s
-            if 0 <= k < steps:
-                if s <= 1 and k == 0:
-                    p1_wait(s)
-                ag_start(s, k)
-            if k == steps:
-                ag_finish(s)
-            r = k - steps - 1
-            if 0 <= r < kz:
-                rs_start(s, r)
-            if r == kz:
-                rs_finish(s)
-        if t == 0:
+    plan = []
+    for s in range(STAGES):
+        plan += [(k + 0.4 * s, s, ag_start, k) for k in range(steps)]
+        plan += [(steps + 0.4 * s, s, multiply, None)]
+        plan += [(steps + 1 + 0.4 * s + r, s, rs_start, r) for r in range(kz)]
+        plan += [(steps + 1 + 0.4 * s + kz, s, rs_finish, None)]
+    for _, s, step, k in sorted(plan, key=lambda e: e[:2]):
+        if step is ag_start and k == 0 and s <= 1:
+            p1_wait(s)
+        if k is None:
+            step(s)
+        else:
+            step(s, k)
+        if step is ag_start and k == 0 and s == 2:
             prepare()
-            locals_[2].wait()
-        for s in range(STAGES):
-            if t - 2 * s == steps:
-                compute(s)
-                swap(s).start()
-                if s == STAGES - 1:
-                    finish_slots()
+        if step is rs_start and k == min(1, kz - 1):
+            backs(s)
+            if s == STAGES - 1:
+                finish_slots()
     finish_dots()
 
     for path, k in p1_all:
@@ -370,12 +406,15 @@
         for k in range(steps):
             for p, r in streams(k):
                 ag(s, k, p, r).wait_send()
-        swap(s).wait_send()
+        for part in (0, 1):
+            swap(s, part).wait_send()
         for r in range(kz):
             for right in (True, False):
                 rs(s, r, right).wait_send()
     for k in range(1, nx):
         dot_copy(k).wait_send()
+    for c in slot_copies + [down_copy(s) for s in range(STAGES)]:
+        c.wait()
 
 
 def solution(mesh):
@@ -390,18 +429,21 @@
         kz = nz // 2
         dma = pltpu.SemaphoreType.DMA
         vmem = pl.BlockSpec(memory_space=pltpu.VMEM)
-        hbm = pl.BlockSpec(memory_space=pl.ANY)
-        return pl.pallas_call(
+        hbm = pl.BlockSpec(memory_space=pltpu.HBM)
+        outs = pl.pallas_call(
             functools.partial(kernel, nx, ny, nz),
             out_shape=(
                 jax.ShapeDtypeStruct(pre_gate.shape, BF16),
                 jax.ShapeDtypeStruct(pre_up.shape, BF16),
-                jax.ShapeDtypeStruct((1, hidden, width // (2 * nz)), F32),
+                jax.ShapeDtypeStruct((1, width // (2 * nz), hidden), F32),
                 jax.ShapeDtypeStruct((1, rows), F32),
             ),
-            in_specs=[vmem, vmem, vmem, hbm, hbm, hbm],
-            out_specs=(vmem, vmem, vmem, vmem),
+            in_specs=[hbm] * 6,
+            out_specs=(hbm, hbm, hbm, vmem),
             scratch_shapes=[
+                pltpu.VMEM(grad_out.shape, BF16),
+                pltpu.VMEM(expert_ids.shape[::-1], jnp.int32),
+                pltpu.VMEM(gate_values.shape[::-1], BF16),
                 pltpu.VMEM((nx, ny, SLAB, LANE), BF16),
                 pltpu.VMEM((nx, ny, SLAB, LANE), BF16),
                 pltpu.VMEM((ny, tok, LANE), BF16),
@@ -409,7 +451,6 @@
                 pltpu.VMEM((rows, hidden), BF16),
                 pltpu.VMEM((rows, hidden), BF16),
                 pltpu.VMEM((rows, hidden), BF16),
-                pltpu.VMEM((rows, rows), BF16),
                 pltpu.VMEM((rows, rows), BF16),
                 pltpu.VMEM((hidden, rows), BF16),
                 pltpu.VMEM((rows, hidden), BF16),
@@ -426,24 +467,29 @@
                 pltpu.VMEM((kz, 2, half, hidden), BF16),
                 pltpu.VMEM((kz, 2, half, hidden), BF16),
                 pltpu.VMEM((nx, 8, rows), F32),
-                dma((3,)),
+                pltpu.VMEM((rows, hidden), BF16),
+                pltpu.VMEM((rows, hidden), BF16),
+                pltpu.VMEM((STAGES, LANE, hidden), F32),
+                dma((6,)),
+                dma((6,)),
                 dma((2, 2, max(nx, ny))),
                 dma((2, 2, max(nx, ny))),
                 dma((ny,)),
                 dma((ny,)),
                 dma((STAGES, steps, 2, 2)),
                 dma((STAGES, steps, 2, 2)),
-                dma((STAGES,)),
-                dma((STAGES,)),
+                dma((STAGES, 2)),
+                dma((STAGES, 2)),
                 dma((STAGES, kz, 2)),
                 dma((STAGES, kz, 2)),
                 dma((nx,)),
                 dma((nx,)),
             ],
             compiler_params=pltpu.CompilerParams(
-                collective_id=0, has_side_effects=True, vmem_limit_bytes=48 * 1024 * 1024
+                collective_id=0, has_side_effects=True, vmem_limit_bytes=60 * 1024 * 1024
             ),
-        )(grad_out, expert_ids, gate_values, pre_gate, pre_up, down_weight)
+        )(grad_out, expert_ids.T, gate_values.T, pre_gate, pre_up, down_weight)
+        return outs[0], outs[1], jnp.swapaxes(outs[2], 1, 2), outs[3]
 
     placed = (
         P(("dp", "ep"), "tp"),

time: 99.5 us -> 85.1 us (0.86)
  the two profiles are of different devices: /device:TPU:2 before, /device:TPU:6 now
where the time goes in v2:
time: 85.1 us; the launch traced here: 84.9 us
  Pallas kernels  78.1 us (92%)
  local copies, waits for them, and re-layouts  6.18 us (7%)
    pallas_call x1, Pallas kernels, local(): pl.pallas_call(functools.partial(kernel, nx, ny, nz), out_shape=(jax.Shap...  78.1 us
    unnamed x4, local copies, waits for them, and re-layouts  6.18 us

profile of v2, /device:TPU:6, one launch (start us, length us, event | category | flops | bytes accessed | tf_op | source)
XLA Modules:
  0.0 84.9 jit_solution(14677186681077769614)
XLA Ops:
  0.6 78.1 %shard_map.93 = (bf16[1,256,256]{2,1,0:T(8,128)(2,1)}, bf16[1,256,256]{2,1,0:T(8,128)(2,1)}, f32[1,448,256]{2,1,0:T(8,128)}, f32[1,256]{1,0:T(1,128)}) custom-call(bf16[32,896]{1,0:T(8,128)(2,1)} %grad_hbm.1, s32[4,32]{1,0:T(4,128)} %bitcast.4, bf16[4,32]{1,0:T(4,128)(2,1)} %bitcast.5, bf16[1,256,256]{2,1,0:T(8,128)(2,1)} %pg_hbm.1, ...), custom_call_target="tpu_custom_call" | custom-call | tf_op jit(solution)/shard_map/pallas_call | solution.py:433
  78.7 1.6 %copy.14 = bf16[1,256,256]{2,1,0:T(8,128)(2,1)} copy(bf16[1,256,256]{2,1,0:T(8,128)(2,1)} %get-tuple-element.16) | data formatting | bytes 262144
  80.3 1.6 %copy.15 = bf16[1,256,256]{2,1,0:T(8,128)(2,1)} copy(bf16[1,256,256]{2,1,0:T(8,128)(2,1)} %get-tuple-element.17) | data formatting | bytes 262144
  81.8 1.8 %copy.16 = f32[1,256,448]{1,2,0:T(8,128)} copy(f32[1,256,448]{1,2,0:T(8,128)} %bitcast.3) | data formatting | bytes 917504
  83.7 1.2 %copy.17 = f32[1,256]{1,0:T(1,128)} copy(f32[1,256]{1,0:T(1,128)} %get-tuple-element.19) | data formatting | bytes 2048

commit v3 on v2

--- a/solution.py
+++ b/solution.py
@@ -23,12 +23,12 @@
 def kernel(
     nx, ny, nz,
     grad_hbm, ids_hbm, gate_hbm, pg_hbm, pu_hbm, w_hbm,
-    dpg_hbm, dpu_hbm, down_hbm, dgate_ref,
+    dpg_ref, dpu_ref, down_ref, dgate_ref,
     grad_ref, ids_ref, gate_ref,
     ta, tb, meta, w, pg, pu, act, sm, at, am, gslot, back,
     own, away, mate, own3, away3, mate3,
-    out_r, in_r, out_3, in_3, dots, dpg_ref, dpu_ref, down_ref,
-    sem_local, sem_out, p1_send, p1_recv, meta_send, meta_recv,
+    out_r, in_r, out_3, in_3, dots,
+    sem_local, p1_send, p1_recv, meta_send, meta_recv,
     ag_send, ag_recv, mate_send, mate_recv, rs_send, rs_recv, dot_send, dot_recv,
 ):
     tok = grad_ref.shape[0]
@@ -216,20 +216,24 @@
                 own3[i] = mine
                 away3[i] = theirs
             return carry
-        lax.fori_loop(lo, hi, body, 0)
+        lax.fori_loop(lo, hi, body, 0, unroll=True)
 
     def backs(s):
-        def body(i, carry):
-            block = columns(s, i)
-            base = i * 7 * LANE
-            first = pl.multiple_of(base + s * LANE, LANE)
-            weights = w[:, pl.ds(first, LANE)]
-            if s < 3:
-                second = pl.multiple_of(base + (s + 4) * LANE, LANE)
-                weights = jnp.concatenate([weights, w[:, pl.ds(second, LANE)]], axis=1)
-            back[...] += dot(block, weights, ((1,), (1,)))
+        group = min(4, nx)
+
+        def body(g, carry):
+            blocks, weights = [], []
+            for j in range(group):
+                i = g * group + j
+                blocks.append(columns(s, i))
+                for tile in (s, s + 4) if s < 3 else (s,):
+                    first = pl.multiple_of(i * 7 * LANE + tile * LANE, LANE)
+                    weights.append(w[:, pl.ds(first, LANE)])
+            back[...] += dot(
+                jnp.concatenate(blocks, axis=1), jnp.concatenate(weights, axis=1), ((1,), (1,))
+            )
             return carry
-        lax.fori_loop(0, nx, body, 0)
+        lax.fori_loop(0, nx // group, body, 0)
 
     cut = min(3, nx - 1)
 
@@ -309,25 +313,11 @@
             parts.append(value)
         value = jnp.concatenate(parts, axis=0)
         if s < 3:
-            down_ref[s] = value.T
-            down_copy(s).start()
+            first = pl.multiple_of(LANE * s + core * (LANE // 2), 8)
+            down_ref[0, pl.ds(first, LANE), :] = value.T
         else:
-            down_ref[s, 0:LANE // 2, :] = value
-            down_copy(s).start()
-
-    def down_copy(s):
-        first = LANE * s + core * (LANE // 2) if s < 3 else (1 - core) * 3 * LANE
-        size = LANE if s < 3 else LANE // 2
-        return pltpu.make_async_copy(
-            down_ref.at[s, pl.ds(0, size), :],
-            down_hbm.at[0, pl.ds(pl.multiple_of(first, 8), size), :],
-            sem_out.at[s],
-        )
-
-    slot_copies = [
-        pltpu.make_async_copy(dpg_ref, dpg_hbm.at[0], sem_out.at[4]),
-        pltpu.make_async_copy(dpu_ref, dpu_hbm.at[0], sem_out.at[5]),
-    ]
+            first = pl.multiple_of((1 - core) * 3 * LANE, 8)
+            down_ref[0, pl.ds(first, LANE // 2), :] = value
 
     def dot_copy(k):
         return pltpu.make_async_remote_copy(
@@ -350,10 +340,8 @@
         up_pre = pu[...].astype(F32)
         sigma = jax.nn.sigmoid(gate_pre)
         grad_act = gslot[...] * placed
-        dpg_ref[...] = (grad_act * up_pre * sigma * (1.0 + gate_pre * (1.0 - sigma))).astype(BF16)
-        dpu_ref[...] = (grad_act * (gate_pre * sigma)).astype(BF16)
-        for c in slot_copies:
-            c.start()
+        dpg_ref[0] = (grad_act * up_pre * sigma * (1.0 + gate_pre * (1.0 - sigma))).astype(BF16)
+        dpu_ref[0] = (grad_act * (gate_pre * sigma)).astype(BF16)
 
     def finish_dots():
         for k in range(1, nx):
@@ -380,8 +368,8 @@
     for s in range(STAGES):
         plan += [(k + 0.4 * s, s, ag_start, k) for k in range(steps)]
         plan += [(steps + 0.4 * s, s, multiply, None)]
-        plan += [(steps + 1 + 0.4 * s + r, s, rs_start, r) for r in range(kz)]
-        plan += [(steps + 1 + 0.4 * s + kz, s, rs_finish, None)]
+        plan += [(steps + 0.5 + 0.4 * s + r, s, rs_start, r) for r in range(kz)]
+        plan += [(steps + 0.5 + 0.4 * s + kz, s, rs_finish, None)]
     for _, s, step, k in sorted(plan, key=lambda e: e[:2]):
         if step is ag_start and k == 0 and s <= 1:
             p1_wait(s)
@@ -413,8 +401,6 @@
                 rs(s, r, right).wait_send()
     for k in range(1, nx):
         dot_copy(k).wait_send()
-    for c in slot_copies + [down_copy(s) for s in range(STAGES)]:
-        c.wait()
 
 
 def solution(mesh):
@@ -430,16 +416,20 @@
         dma = pltpu.SemaphoreType.DMA
         vmem = pl.BlockSpec(memory_space=pltpu.VMEM)
         hbm = pl.BlockSpec(memory_space=pltpu.HBM)
+        held = [
+            pltpu.with_memory_space_constraint(a, pltpu.HBM)
+            for a in (grad_out, expert_ids.T, gate_values.T, pre_gate, pre_up, down_weight)
+        ]
         outs = pl.pallas_call(
             functools.partial(kernel, nx, ny, nz),
             out_shape=(
-                jax.ShapeDtypeStruct(pre_gate.shape, BF16),
-                jax.ShapeDtypeStruct(pre_up.shape, BF16),
-                jax.ShapeDtypeStruct((1, width // (2 * nz), hidden), F32),
-                jax.ShapeDtypeStruct((1, rows), F32),
+                pltpu.VMEM(pre_gate.shape, BF16),
+                pltpu.VMEM(pre_up.shape, BF16),
+                pltpu.VMEM((1, width // (2 * nz), hidden), F32),
+                pltpu.VMEM((1, rows), F32),
             ),
             in_specs=[hbm] * 6,
-            out_specs=(hbm, hbm, hbm, vmem),
+            out_specs=(vmem,) * 4,
             scratch_shapes=[
                 pltpu.VMEM(grad_out.shape, BF16),
                 pltpu.VMEM(expert_ids.shape[::-1], jnp.int32),
@@ -467,10 +457,6 @@
                 pltpu.VMEM((kz, 2, half, hidden), BF16),
                 pltpu.VMEM((kz, 2, half, hidden), BF16),
                 pltpu.VMEM((nx, 8, rows), F32),
-                pltpu.VMEM((rows, hidden), BF16),
-                pltpu.VMEM((rows, hidden), BF16),
-                pltpu.VMEM((STAGES, LANE, hidden), F32),
-                dma((6,)),
                 dma((6,)),
                 dma((2, 2, max(nx, ny))),
                 dma((2, 2, max(nx, ny))),
@@ -486,9 +472,9 @@
                 dma((nx,)),
             ],
             compiler_params=pltpu.CompilerParams(
-                collective_id=0, has_side_effects=True, vmem_limit_bytes=60 * 1024 * 1024
+                collective_id=0, has_side_effects=True, vmem_limit_bytes=48 * 1024 * 1024
             ),
-        )(grad_out, expert_ids.T, gate_values.T, pre_gate, pre_up, down_weight)
+        )(*held)
         return outs[0], outs[1], jnp.swapaxes(outs[2], 1, 2), outs[3]
 
     placed = (

time: 85.1 us -> 77 us (0.905)
  the two profiles are of different devices: /device:TPU:6 before, /device:TPU:1 now
where the time goes in v3:
time: 77 us; the launch traced here: 76.8 us
  Pallas kernels  73.5 us (95%)
  local copies, waits for them, and re-layouts  2.64 us (3%)
    pallas_call x1, Pallas kernels, local(): pl.pallas_call(functools.partial(kernel, nx, ny, nz), out_shape=(pltpu.VM...  73.5 us
    unnamed x4, local copies, waits for them, and re-layouts  2.64 us

profile of v3, /device:TPU:1, one launch (start us, length us, event | category | flops | bytes accessed | tf_op | source)
XLA Modules:
  0.0 76.8 jit_solution(10008720789707040620)
XLA Ops:
  0.6 73.5 %shard_map.93 = (bf16[1,256,256]{2,1,0:T(8,128)(2,1)S(1)}, bf16[1,256,256]{2,1,0:T(8,128)(2,1)S(1)}, f32[1,448,256]{2,1,0:T(8,128)S(1)}, f32[1,256]{1,0:T(1,128)S(1)}) custom-call(bf16[32,896]{1,0:T(8,128)(2,1)} %grad_hbm.1, s32[4,32]{1,0:T(4,128)} %bitcast.4, bf16[4,32]{1,0:T(4,128)(2,1)} %bitcast.5, bf16[1,256,256]{2,1,0:T(8,128)(2,1)} %pg_hbm.1, ...), custom_call_target="tpu_custom_call" | custom-call | tf_op jit(solution)/shard_map/pallas_call | solution.py:423
  74.1 0.7 copy.14
  74.8 0.6 copy.17
  75.4 0.7 copy.15
  76.0 0.8 copy.16

commit v4 on v3

--- a/solution.py
+++ b/solution.py
@@ -14,6 +14,7 @@
 STAGES = 4
 ROWS = ((0, 32), (32, 32), (64, 32), (96, 16))
 SLAB = 112
+PARTS = ((0, 64), (64, 48))
 
 
 def dot(a, b, dims=((1,), (0,))):
@@ -90,7 +91,7 @@
     pl.semaphore_wait(barrier, len(peers))
 
     def p1(path, part, k):
-        lo, n = (0, 32) if part == 0 else (32, SLAB - 32)
+        lo, n = PARTS[part]
         buf = ta if path == 0 else tb
         ref = buf.at[x, y, pl.ds(lo, n), :]
         return pltpu.make_async_remote_copy(
@@ -112,8 +113,9 @@
         p1(path, 0, k).start()
     for k in range(1, ny):
         meta_copy(k).start()
-    for path, k in p1_all:
-        p1(path, 1, k).start()
+    for part in range(1, len(PARTS)):
+        for path, k in p1_all:
+            p1(path, part, k).start()
 
     def ag(s, k, path, right):
         lo, n = ROWS[s]
@@ -364,6 +366,22 @@
         for path, k in p1_all:
             p1(path, part, k).wait_recv()
 
+    def drain():
+        for path, k in p1_all:
+            for part in range(len(PARTS)):
+                p1(path, part, k).wait_send()
+        for k in range(1, ny):
+            meta_copy(k).wait_send()
+        for s in range(STAGES):
+            for k in range(steps):
+                for p, r in streams(k):
+                    ag(s, k, p, r).wait_send()
+            for part in (0, 1):
+                swap(s, part).wait_send()
+            for r in range(kz - 1):
+                for right in (True, False):
+                    rs(s, r, right).wait_send()
+
     plan = []
     for s in range(STAGES):
         plan += [(k + 0.4 * s, s, ag_start, k) for k in range(steps)]
@@ -371,8 +389,10 @@
         plan += [(steps + 0.5 + 0.4 * s + r, s, rs_start, r) for r in range(kz)]
         plan += [(steps + 0.5 + 0.4 * s + kz, s, rs_finish, None)]
     for _, s, step, k in sorted(plan, key=lambda e: e[:2]):
-        if step is ag_start and k == 0 and s <= 1:
-            p1_wait(s)
+        if step is ag_start and k == 0:
+            for part, (lo, _) in enumerate(PARTS):
+                if lo == ROWS[s][0]:
+                    p1_wait(part)
         if k is None:
             step(s)
         else:
@@ -383,22 +403,13 @@
             backs(s)
             if s == STAGES - 1:
                 finish_slots()
+        if step is rs_start and k == kz - 1 and s == STAGES - 1:
+            drain()
     finish_dots()
 
-    for path, k in p1_all:
-        for part in (0, 1):
-            p1(path, part, k).wait_send()
-    for k in range(1, ny):
-        meta_copy(k).wait_send()
     for s in range(STAGES):
-        for k in range(steps):
-            for p, r in streams(k):
-                ag(s, k, p, r).wait_send()
-        for part in (0, 1):
-            swap(s, part).wait_send()
-        for r in range(kz):
-            for right in (True, False):
-                rs(s, r, right).wait_send()
+        for right in (True, False):
+            rs(s, kz - 1, right).wait_send()
     for k in range(1, nx):
         dot_copy(k).wait_send()
 
@@ -458,8 +469,8 @@
                 pltpu.VMEM((kz, 2, half, hidden), BF16),
                 pltpu.VMEM((nx, 8, rows), F32),
                 dma((6,)),
-                dma((2, 2, max(nx, ny))),
-                dma((2, 2, max(nx, ny))),
+                dma((2, len(PARTS), max(nx, ny))),
+                dma((2, len(PARTS), max(nx, ny))),
                 dma((ny,)),
                 dma((ny,)),
                 dma((STAGES, steps, 2, 2)),

time: 77 us -> 76.1 us (0.988)
  Pallas kernels: 73.5 us -> 72.6 us
    pallas_call x1, Pallas kernels: 73.5 us -> 72.6 us  [local(): pl.pallas_call(functools.partial(kernel, nx, ny, nz), out_shape=(pltpu.VM...]
where the time goes in v4:
time: 76.1 us; the launch traced here: 75.9 us
  Pallas kernels  72.6 us (95%)
  local copies, waits for them, and re-layouts  2.64 us (3%)
    pallas_call x1, Pallas kernels, local(): pl.pallas_call(functools.partial(kernel, nx, ny, nz), out_shape=(pltpu.VM...  72.6 us
    unnamed x4, local copies, waits for them, and re-layouts  2.64 us

profile of v4, /device:TPU:1, one launch (start us, length us, event | category | flops | bytes accessed | tf_op | source)
XLA Modules:
  0.0 75.9 jit_solution(561363355015539471)
XLA Ops:
  0.6 72.6 %shard_map.93 = (bf16[1,256,256]{2,1,0:T(8,128)(2,1)S(1)}, bf16[1,256,256]{2,1,0:T(8,128)(2,1)S(1)}, f32[1,448,256]{2,1,0:T(8,128)S(1)}, f32[1,256]{1,0:T(1,128)S(1)}) custom-call(bf16[32,896]{1,0:T(8,128)(2,1)} %grad_hbm.1, s32[4,32]{1,0:T(4,128)} %bitcast.4, bf16[4,32]{1,0:T(4,128)(2,1)} %bitcast.5, bf16[1,256,256]{2,1,0:T(8,128)(2,1)} %pg_hbm.1, ...), custom_call_target="tpu_custom_call" | custom-call | tf_op jit(solution)/shard_map/pallas_call | solution.py:434
  73.3 0.7 copy.14
  73.9 0.6 copy.17
  74.5 0.7 copy.15
  75.2 0.8 %copy.16 = f32[1,256,448]{1,2,0:T(8,128)} copy(f32[1,256,448]{1,2,0:T(8,128)S(1)} %bitcast.3) | data formatting | bytes 917504
